TPU v7x, 32 devices: a whole 2x2x4 slice. The times are simulated.
32 devices in a mesh: groups: 2 (over x), sector: 16 (over z, y, core).
Axes of the slice: x: 2, y: 2, z: 4, core: 2. Of those that a mesh axis runs over, the one named last changes fastest.
Arguments:
- wave_blocks: bfloat16 [256, 128, 128], P(('groups', 'sector')), parts along dimension 0, may hold values from -6 to 6
- davidson_basis: bfloat16 [4, 256, 128, 128], P(None, ('groups', 'sector')), parts along dimension 1
- left_env: bfloat16 [128, 128, 16, 128], P(('groups', 'sector')), parts along dimension 0, may hold values from -0.125 to 0.125
- right_env: bfloat16 [128, 128, 16, 128], P(('groups', 'sector')), parts along dimension 0, may hold values from -0.25 to 0.25
- source_owner: int32 [512, 1], P('groups'), parts along dimension 0, may hold values from 0 to 15; in each aligned block of 16 rows (0 to 15, 16 to 31, ...) at most 2 rows name the same one
- source_slot: int32 [512], P('groups'), parts along dimension 0, may hold values from 0 to 7
- target_owner: int32 [512, 1], P('groups'), parts along dimension 0, may hold values from 0 to 15; in each aligned block of 16 rows (0 to 15, 16 to 31, ...) at most 2 rows name the same one
- target_slot: int32 [512], P('groups'), parts along dimension 0, may hold values from 0 to 7
Outputs:
- applied: bfloat16 [256, 128, 128], P(('groups', 'sector')), parts along dimension 0
- correlations: float32 [8], P('groups'), parts along dimension 0
There are 2 independent parts, one for each index of `groups`. A program takes and returns all parts, laid end to end along the dimension named above; each array names one. Nothing has to cross between parts.
Inputs may be any that keep to these rules, and one draw needn't show every extreme that they name: `source_owner`: among the 16 rows of one task device no owner appears more than 2 times. `target_owner`: among the 16 rows of one task device no owner appears more than 2 times.
All inputs are finite; a program needn't handle non-finite values.
Results may differ from a plain program's by a relative error of at most 0.0062.
Values may be sent and summed in bfloat16 or wider, within the bound.
A program may use at most 64 MiB of HBM per device.

v0:
```python
import jax
import jax.numpy as jnp
from jax import lax
from jax.sharding import PartitionSpec as P

CAP = 2


def slot_table(owner_rows, myself, capacity):
    matches = (owner_rows == myself).astype(jnp.int32)
    placed = jnp.cumsum(matches, axis=1) - 1
    wanted = jnp.arange(capacity, dtype=jnp.int32)
    return (matches[:, None, :] == 1) & (placed[:, None, :] == wanted[None, :, None])


def own_ranks(owners, members):
    columns = jnp.arange(members, dtype=jnp.int32)
    matches = (owners[:, None] == columns[None, :]).astype(jnp.int32)
    placed = jnp.cumsum(matches, axis=0) - 1
    return jnp.sum(matches * placed, axis=1)


def shards(
    wave_blocks,
    davidson_basis,
    left_env,
    right_env,
    source_owner,
    source_slot,
    target_owner,
    target_slot,
):
    members = lax.axis_size("sector")
    myself = lax.axis_index("sector")
    owned = wave_blocks.shape[0]
    width = wave_blocks.shape[1]
    right_count = right_env.shape[0]
    needed = source_slot.shape[0] // members
    produced = target_slot.shape[0] // members
    repeats = needed // right_count
    capacity = CAP
    my_owners = lax.dynamic_slice_in_dim(source_owner[:, 0], myself * needed, needed)
    everything = lax.all_gather(wave_blocks, "sector", axis=0, tiled=True)
    my_slots = lax.dynamic_slice_in_dim(source_slot, myself * needed, needed)
    inputs = everything[my_owners * owned + my_slots]
    inputs = inputs.reshape(right_count, repeats, width, width)
    contracted = jnp.einsum(
        "bclr,brws->cwls", inputs, right_env, preferred_element_type=jnp.float32
    ).astype(jnp.bfloat16)
    results = jnp.einsum(
        "axwl,cwls->acxs", left_env, contracted, preferred_element_type=jnp.float32
    ).astype(jnp.bfloat16)
    results = results.reshape(produced, width, width)
    my_targets = lax.dynamic_slice_in_dim(target_owner[:, 0], myself * produced, produced)
    target_ranks = own_ranks(my_targets, members)
    columns = jnp.arange(members, dtype=jnp.int32)
    wanted = jnp.arange(capacity, dtype=jnp.int32)
    rows_here = jnp.arange(produced, dtype=jnp.int32)
    selects = (my_targets[None, None, :] == columns[:, None, None]) & (
        target_ranks[None, None, :] == wanted[None, :, None]
    )
    back_index = jnp.sum(selects * rows_here[None, None, :], axis=2)
    returned = lax.all_to_all(
        results[back_index], "sector", split_axis=0, concat_axis=0, tiled=True
    )
    owner_picks = slot_table(target_owner[:, 0].reshape(members, produced), myself, capacity)
    landing = jnp.sum(owner_picks * target_slot.reshape(members, produced)[:, None, :], axis=2)
    filled = jnp.any(owner_picks, axis=2)
    block_ids = jnp.arange(owned, dtype=jnp.int32)
    assign = (
        (landing.reshape(-1)[None, :] == block_ids[:, None]) & filled.reshape(-1)[None, :]
    ).astype(jnp.bfloat16)
    summed = jnp.dot(
        assign,
        returned.reshape(members * capacity, width * width),
        preferred_element_type=jnp.float32,
    )
    applied = summed.reshape(owned, width, width).astype(jnp.bfloat16)
    partial_value = jnp.einsum(
        "vbxy,bxy->v", davidson_basis, applied, preferred_element_type=jnp.float32
    )
    correlations = lax.psum(partial_value, "sector")
    return (applied, correlations)


def solution(mesh):
    return jax.shard_map(
        shards,
        mesh=mesh,
        in_specs=(
            P(("groups", "sector"), None, None),
            P(None, ("groups", "sector"), None, None),
            P(("groups", "sector"), None, None, None),
            P(("groups", "sector"), None, None, None),
            P("groups", None),
            P("groups"),
            P("groups", None),
            P("groups"),
        ),
        out_specs=(P(("groups", "sector"), None, None), P("groups")),
        check_vma=False,
    )
```

profile of v0, /device:TPU:0, one launch (start us, length us, event | category | flops | bytes accessed | tf_op | source)
XLA Modules:
  0.0 144.9 jit_solution(16344387261705797452)
XLA Ops:
  7.2 0.0 copy-start
  7.2 0.0 all-gather.2.cloned.1.call-start
  7.2 0.7 all-gather.2.cloned.1.call-update
  7.9 0.7 dynamic-slice_bitcast_fusion
  8.6 0.1 iota_compare_fusion.2
  8.8 0.2 select_reduce_fusion.2
  9.0 0.1 select_reduce_fusion
  9.1 0.1 copy.33
  9.2 0.1 reshape.121
  9.3 0.8 compare_select_fusion.1
  10.1 53.4 %all-gather.2.cloned.1.call-done = bf16[128,128,128]{2,1,0:T(8,128)(2,1)} async-done(((bf16[8,128,128]{2,1,0:T(8,128)(2,1)}), bf16[128,128,128]{2,1,0:T(8,128)(2,1)}) %all-gather.2.cloned.1.call-update) | async-done | bytes 4194320 | tf_op jit(solution)/shard_map/all_gather | solution.py:43
  63.5 2.8 %gather_fusion = bf16[16,128,128]{2,1,0:T(8,128)(2,1)S(1)} fusion(bf16[128,128,128]{2,1,0:T(8,128)(2,1)} %all-gather.2.cloned.1.call-done, s32[1024]{0:T(1024)S(1)} %pad_clamp_fusion.1), kind=kCustom, calls=%fused_computation | custom fusion | bytes 1048640 | tf_op jit(solution)/shard_map/gather | solution.py:45
  66.3 4.6 %fusion.16 = bf16[4,4,128,128]{2,3,0,1:T(8,128)(2,1)S(1)} fusion(bf16[4,128,16,128]{3,2,1,0:T(8,128)(2,1)} %param.10, bf16[4,128,16,128]{3,2,1,0:T(8,128)(2,1)} %param.11, bf16[4,4,128,128,1]{3,2,1,0,4:T(8,128)(2,1)S(1)} %bitcast.84), kind=kOutput, calls=%fused_computation.11 | convolution fusion | flops 2148794368 | bytes 5242880 | tf_op jit(solution)/shard_map/axwl,cwls->acxs/dot_general | solution.py:50
  70.9 0.3 copy.32
  71.2 0.0 copy-start.2
  71.3 0.0 copy-start.1
  71.3 1.7 %gather_fusion.1 = bf16[32,128,128]{2,1,0:T(8,128)(2,1)} fusion(bf16[16,128,128]{2,1,0:T(8,128)(2,1)S(1)} %bitcast.82, s32[1024]{0:T(1024)S(1)} %pad_clamp_fusion), kind=kCustom, calls=%fused_computation.1 | custom fusion | bytes 2097280 | tf_op jit(solution)/shard_map/gather | solution.py:64
  72.9 3.7 %all-to-all-start = ((bf16[16,2,128,128]{3,2,1,0:T(8,128)(2,1)}), bf16[16,2,128,128]{3,2,1,0:T(8,128)(2,1)S(1)}, u32[]{:S(2)}, u32[]{:S(2)}) async-start(bf16[16,2,128,128]{3,2,1,0:T(8,128)(2,1)} %bitcast.16), calls=%async_computation | async-start | bytes 2097152 | tf_op jit(solution)/shard_map/all_to_all | solution.py:63
  76.6 0.0 copy-done.2
  76.6 0.1 reshape.110
  76.7 0.2 reduce_window_sum.22
  76.9 0.1 fusion.32
  77.0 0.1 copy.27
  77.1 0.1 and.34
  77.2 0.0 copy-done.1
  77.2 0.1 mul.32
  77.3 0.1 select_reduce_fusion.1
  77.4 0.1 copy.26
  77.5 0.1 eq.112
  77.6 21.9 %all-to-all-done = bf16[16,2,128,128]{3,2,1,0:T(8,128)(2,1)S(1)} async-done(((bf16[16,2,128,128]{3,2,1,0:T(8,128)(2,1)}), bf16[16,2,128,128]{3,2,1,0:T(8,128)(2,1)S(1)}, u32[]{:S(2)}, u32[]{:S(2)}) %all-to-all-start) | async-done | bytes 1048608 | tf_op jit(solution)/shard_map/all_to_all | solution.py:63
  99.5 0.7 convolution_convert_fusion
  100.2 0.0 copy-done
  100.2 1.8 %convolution_bitcast_fusion = f32[4]{0:T(128)S(1)} fusion(bf16[4,8,128,128]{3,2,1,0:T(8,128)(2,1)S(1)} %copy-done, bf16[8,128,128,1]{2,0,1,3:T(8,128)(2,1)S(1)} %bitcast.85), kind=kOutput, calls=%fused_computation.13 | convolution fusion | flops 1048576 | bytes 1310736 | tf_op jit(solution)/shard_map/vbxy,bxy->v/dot_general | solution.py:79
  102.0 0.8 copy.35
  102.7 35.3 %psum.7 = f32[4]{0:T(128)} all-reduce(f32[4]{0:T(128)S(1)} %convolution_bitcast_fusion), channel_id=1, replica_groups=mesh['groups'=2,'sector'=16] {'sector'}, use_global_device_ids=true, to_apply=%region_6.7 | all-reduce | flops 4 | bytes 32 | tf_op jit(solution)/shard_map/psum | solution.py:82
  (8 shorter events, 0.1 us)
Async XLA Ops:
  7.2 93.0 %copy-start = (bf16[4,8,128,128]{3,2,1,0:T(8,128)(2,1)S(1)}, bf16[4,8,128,128]{3,2,1,0:T(8,128)(2,1)}, u32[]{:S(2)}) copy-start(bf16[4,8,128,128]{3,2,1,0:T(8,128)(2,1)} %param.9) | copy-start | bytes 3145732
  7.2 56.3 %all-gather.2.cloned.1.call-start = ((), (), s32[]{:S(2)}) async-start(), calls=%async_computation.1 | async-start | bytes 4456448 | tf_op jit(solution)/shard_map/all_gather | solution.py:43
  71.2 5.4 %copy-start.2 = (s32[256,1]{0,1:T(1,128)S(1)}, s32[256,1]{0,1:T(1,128)}, u32[]{:S(2)}) copy-start(s32[256,1]{0,1:T(1,128)} %param.14) | copy-start | bytes 3076
  71.3 6.0 %copy-start.1 = (s32[256]{0:T(256)S(1)}, s32[256]{0:T(256)}, u32[]{:S(2)}) copy-start(s32[256]{0:T(256)} %param.15) | copy-start | bytes 3076
  72.9 26.6 %all-to-all-start = ((bf16[16,2,128,128]{3,2,1,0:T(8,128)(2,1)}), bf16[16,2,128,128]{3,2,1,0:T(8,128)(2,1)S(1)}, u32[]{:S(2)}, u32[]{:S(2)}) async-start(bf16[16,2,128,128]{3,2,1,0:T(8,128)(2,1)} %bitcast.16), calls=%async_computation | async-start | bytes 2097152 | tf_op jit(solution)/shard_map/all_to_all | solution.py:63
Sparse Core Ops, SparseCore 0:
  10.2 53.2 all-gather.1
where the time goes:
time: 145 us
  waiting for transfers between devices  76 us (52%)
  blocking collectives  35.3 us (24%)
  between operations  14.1 us (10%)
  matrix products  7.08 us (5%)
  local copies, waits for them, and re-layouts  7.04 us (5%)
  starting transfers between devices  3.69 us (3%)
  other arithmetic  1.64 us (1%)
    all_gather x1, waiting for transfers between devices, shards(): everything = lax.all_gather(wave_blocks, 'sector', axis=0, tiled=True)  53.4 us
    psum x1, blocking collectives, shards(): correlations = lax.psum(partial_value, 'sector')  35.3 us
    all_to_all x1, waiting for transfers between devices, shards(): lax.all_to_all(results[back_index], 'sector', split_axis=0, concat_axis=0...  21.9 us
    dot_general x1, matrix products, shards(): jnp.einsum('axwl,cwls->acxs', left_env, contracted, preferred_element_typ...  4.6 us
    all_to_all x1, starting transfers between devices, shards(): lax.all_to_all(results[back_index], 'sector', split_axis=0, concat_axis=0...  3.65 us
  transfers between devices with their start and end apart: 2, of which 2 were waited for; matrix products, arithmetic and copies ran while one was open for 2% of the time, Pallas kernels for 0%

commit v1 on v0

v1 whole, which is shorter than its diff:
```python
import functools

import jax
import jax.numpy as jnp
from jax import lax
from jax.experimental import pallas as pl
from jax.experimental.pallas import tpu as pltpu
from jax.sharding import PartitionSpec as P

CAP = 2
CHUNKS = 2
MESH = pl.DeviceIdType.MESH


def two_hits(owner_ref, base, rows, who, value, default):
    def step(at, found):
        first, second = found
        row = rows - 1 - at
        hit = owner_ref[base + row] == who
        return jnp.where(hit, value(row), first), jnp.where(hit, first, second)

    start = (jnp.int32(default), jnp.int32(default))
    return lax.fori_loop(0, rows, step, start, unroll=16)


def kernel(
    n,
    repeats,
    sown,
    sslot,
    town,
    tslot,
    wave_hbm,
    dav_hbm,
    left_hbm,
    right_hbm,
    applied_ref,
    corr_ref,
    wave,
    dav,
    raw_r,
    raw_l,
    flat_r,
    flat_l,
    in_send0,
    in_send1,
    in_recv0,
    in_recv1,
    operand,
    contracted,
    res0,
    res1,
    out_send0,
    out_send1,
    out_recv0,
    out_recv1,
    acc,
    corr_part,
    corr_send,
    corr_recv,
    landing,
    load_sem,
    right_sem,
    left_sem,
    in_ssem,
    in_rsem,
    out_ssem,
    out_rsem,
    corr_ssem,
    corr_rsem,
):
    me = lax.axis_index("sector")
    rows = sslot.shape[0] // n
    owned, width = wave.shape[0], wave.shape[1]
    envs = right_hbm.shape[0]
    terms = right_hbm.shape[2]
    nv = dav.shape[0]
    part = width // CHUNKS
    in_send, in_recv = (in_send0, in_send1), (in_recv0, in_recv1)
    res = (res0, res1)
    out_send, out_recv = (out_send0, out_send1), (out_recv0, out_recv1)

    def peer(t):
        off = n // 2 + (1 - 2 * (t % 2)) * ((t + 1) // 2)
        return lax.rem(me + off, n)

    def source(t):
        off = n // 2 + (1 - 2 * (t % 2)) * ((t + 1) // 2)
        return lax.rem(me - off + n, n)

    load_wave = pltpu.make_async_copy(wave_hbm, wave, load_sem.at[0])
    load_dav = pltpu.make_async_copy(dav_hbm, dav, load_sem.at[1])

    def load_right(b):
        return pltpu.make_async_copy(right_hbm.at[b], raw_r.at[b], right_sem.at[b])

    def load_left(a):
        return pltpu.make_async_copy(left_hbm.at[a], raw_l.at[a], left_sem.at[a])

    load_wave.start()
    for b in range(envs):
        load_right(b).start()
    for a in range(envs):
        load_left(a).start()
    load_dav.start()

    barrier = pltpu.get_barrier_semaphore()

    @pl.loop(0, n - 1)
    def _(t):
        pl.semaphore_signal(
            barrier, inc=1, device_id={"sector": peer(t)}, device_id_type=MESH
        )

    load_wave.wait()

    def pick(p):
        return two_hits(sown, p * rows, rows, me, lambda row: sslot[p * rows + row], 0)

    own0, own1 = pick(me)
    for k, slot in enumerate((own0, own1)):
        for q in range(CHUNKS):
            in_recv[q][me, k] = wave[slot, q * part : (q + 1) * part, :]

    pl.semaphore_wait(barrier, n - 1)

    def in_copy(q, to, frm):
        return pltpu.make_async_remote_copy(
            src_ref=in_send[q].at[to],
            dst_ref=in_recv[q].at[frm],
            send_sem=in_ssem.at[q, to],
            recv_sem=in_rsem.at[q, frm],
            device_id={"sector": to},
            device_id_type=MESH,
        )

    @pl.loop(0, n - 1)
    def _(t):
        p = peer(t)
        slots = pick(p)
        for k in range(CAP):
            for q in range(CHUNKS):
                in_send[q][p, k] = wave[slots[k], q * part : (q + 1) * part, :]
        in_copy(0, p, me).start()

    @pl.loop(0, n - 1)
    def _(t):
        in_copy(1, peer(t), me).start()

    tile = 16
    for b in range(envs):
        load_right(b).wait()

    @pl.loop(0, envs * width // tile)
    def _(i):
        b = i // (width // tile)
        r = (i % (width // tile)) * tile
        r = pl.multiple_of(r, tile)
        block = jnp.swapaxes(raw_r[b, pl.ds(r, tile)], 0, 1)
        for w in range(terms):
            flat_r[pl.ds(pl.multiple_of(b * width + r, tile), tile), w * width : (w + 1) * width] = block[w]

    for a in range(envs):
        load_left(a).wait()

    @pl.loop(0, envs * width // tile)
    def _(i):
        a = i // (width // tile)
        x = (i % (width // tile)) * tile
        x = pl.multiple_of(x, tile)
        q = x // part
        block = jnp.swapaxes(raw_l[a, pl.ds(x, tile)], 0, 1)
        at = pl.multiple_of(q * envs * part + a * part + x % part, tile)
        for w in range(terms):
            flat_l[pl.ds(at, tile), w * width : (w + 1) * width] = block[w]

    @pl.loop(0, n)
    def _(j):
        hits = two_hits(town, j * rows, rows, me, lambda row: tslot[j * rows + row], -1)
        for k in range(CAP):
            landing[j * CAP + k] = hits[k]

    acc[...] = jnp.zeros_like(acc)
    load_dav.wait()

    for q in range(CHUNKS):

        @pl.loop(0, n - 1)
        def _(t):
            in_copy(q, source(t), source(t)).wait_recv()

        @pl.loop(0, rows)
        def _(i):
            owner = sown[me * rows + i]

            def count(h, seen):
                same = (sown[me * rows + h] == owner) & (h < i)
                return seen + same.astype(jnp.int32)

            rank = lax.fori_loop(0, rows, count, jnp.int32(0), unroll=16)
            b = i // repeats
            c = i % repeats
            operand[
                pl.ds(pl.multiple_of(c * part, part), part),
                pl.ds(pl.multiple_of(b * width, width), width),
            ] = in_recv[q][owner, jnp.minimum(rank, CAP - 1)]

        @pl.loop(0, terms // 2)
        def _(pair):
            cols = pl.ds(pl.multiple_of(pair * 2 * width, 2 * width), 2 * width)
            out = jnp.dot(
                operand[...], flat_r[:, cols], preferred_element_type=jnp.float32
            ).astype(jnp.bfloat16)
            for c in range(repeats):
                for h in range(2):
                    at = pl.multiple_of((pair * 2 + h) * width + q * part, part)
                    contracted[pl.ds(at, part), c * width : (c + 1) * width] = out[
                        c * part : (c + 1) * part, h * width : (h + 1) * width
                    ]

    def out_copy(q, to, frm):
        return pltpu.make_async_remote_copy(
            src_ref=out_send[q].at[to],
            dst_ref=out_recv[q].at[frm],
            send_sem=out_ssem.at[q, to],
            recv_sem=out_rsem.at[q, frm],
            device_id={"sector": to},
            device_id_type=MESH,
        )

    for q in range(CHUNKS):
        lhs_rows = slice(q * envs * part, (q + 1) * envs * part)

        @pl.loop(0, repeats // 2)
        def _(pair):
            cols = pl.ds(pl.multiple_of(pair * 2 * width, 2 * width), 2 * width)
            out = jnp.dot(
                flat_l[lhs_rows, :], contracted[:, cols], preferred_element_type=jnp.float32
            ).astype(jnp.bfloat16)
            for a in range(envs):
                for h in range(2):
                    res[q][a * repeats + pair * 2 + h] = out[
                        a * part : (a + 1) * part, h * width : (h + 1) * width
                    ]

        def choose(p):
            return two_hits(town, me * rows, rows, p, lambda row: row, 0)

        @pl.loop(0, n - 1)
        def _(t):
            p = peer(t)
            picked = choose(p)
            for k in range(CAP):
                out_send[q][p, k] = res[q][picked[k]]
            out_copy(q, p, me).start()

        picked = choose(me)
        for k in range(CAP):
            out_recv[q][me, k] = res[q][picked[k]]

    def add(q, j):
        values = [out_recv[q][j, k].astype(jnp.float32) for k in range(CAP)]
        lands = [landing[j * CAP + k] for k in range(CAP)]
        for d in range(owned):
            total = acc[q, d]
            for k in range(CAP):
                total = total + jnp.where(lands[k] == d, 1.0, 0.0) * values[k]
            acc[q, d] = total

    partial = [jnp.zeros((8, width), jnp.float32) for _ in range(nv)]
    for q in range(CHUNKS):
        add(q, me)

        @pl.loop(0, n - 1)
        def _(t):
            j = source(t)
            out_copy(q, j, j).wait_recv()
            add(q, j)

        for d in range(owned):
            block = acc[q, d].astype(jnp.bfloat16)
            applied_ref[d, q * part : (q + 1) * part, :] = block
            block = block.astype(jnp.float32)
            for v in range(nv):
                prod = dav[v, d, q * part : (q + 1) * part, :].astype(jnp.float32) * block
                partial[v] = partial[v] + jnp.sum(prod.reshape(part // 8, 8, width), axis=0)

    for v in range(nv):
        corr_send[v : v + 1, :] = jnp.sum(partial[v], axis=0, keepdims=True)
    if nv < corr_send.shape[0]:
        corr_send[nv:, :] = jnp.zeros((corr_send.shape[0] - nv, width), jnp.float32)

    def corr_copy(to, frm):
        return pltpu.make_async_remote_copy(
            src_ref=corr_send,
            dst_ref=corr_recv.at[frm],
            send_sem=corr_ssem.at[to],
            recv_sem=corr_rsem.at[frm],
            device_id={"sector": to},
            device_id_type=MESH,
        )

    @pl.loop(0, n - 1)
    def _(t):
        corr_copy(peer(t), me).start()

    corr_recv[me] = corr_send[...]

    @pl.loop(0, n - 1)
    def _(t):
        p = peer(t)
        for q in range(CHUNKS):
            in_copy(q, p, me).wait_send()
            out_copy(q, p, me).wait_send()

    @pl.loop(0, n - 1)
    def _(t):
        corr_copy(source(t), source(t)).wait_recv()

    total = jnp.sum(corr_recv[...], axis=0)
    for v in range(nv):
        corr_ref[v] = jnp.sum(total[v : v + 1, :])

    @pl.loop(0, n - 1)
    def _(t):
        corr_copy(peer(t), me).wait_send()


def shards(
    wave_blocks,
    davidson_basis,
    left_env,
    right_env,
    source_owner,
    source_slot,
    target_owner,
    target_slot,
):
    n = lax.axis_size("sector")
    owned, width = wave_blocks.shape[0], wave_blocks.shape[1]
    envs, terms = right_env.shape[0], right_env.shape[2]
    rows = source_slot.shape[0] // n
    repeats = rows // envs
    nv = davidson_basis.shape[0]
    part = width // CHUNKS
    corr_rows = -(-nv // 8) * 8
    bf16 = jnp.bfloat16
    smem = pl.BlockSpec(memory_space=pltpu.SMEM)
    vmem = pl.BlockSpec(memory_space=pltpu.VMEM)
    hbm = pl.BlockSpec(memory_space=pl.ANY)
    dma = pltpu.SemaphoreType.DMA
    flops = 4 * rows * terms * width**3
    return pl.pallas_call(
        functools.partial(kernel, n, repeats),
        out_shape=(
            jax.ShapeDtypeStruct((owned, width, width), bf16),
            jax.ShapeDtypeStruct((nv,), jnp.float32),
        ),
        in_specs=[smem] * 4 + [hbm] * 4,
        out_specs=(vmem, smem),
        scratch_shapes=[
            pltpu.VMEM((owned, width, width), bf16),
            pltpu.VMEM((nv, owned, width, width), bf16),
            pltpu.VMEM((envs, width, terms, width), bf16),
            pltpu.VMEM((envs, width, terms, width), bf16),
            pltpu.VMEM((envs * width, terms * width), bf16),
            pltpu.VMEM((envs * width, terms * width), bf16),
            pltpu.VMEM((n, CAP, part, width), bf16),
            pltpu.VMEM((n, CAP, part, width), bf16),
            pltpu.VMEM((n, CAP, part, width), bf16),
            pltpu.VMEM((n, CAP, part, width), bf16),
            pltpu.VMEM((repeats * part, envs * width), bf16),
            pltpu.VMEM((terms * width, repeats * width), bf16),
            pltpu.VMEM((rows, part, width), bf16),
            pltpu.VMEM((rows, part, width), bf16),
            pltpu.VMEM((n, CAP, part, width), bf16),
            pltpu.VMEM((n, CAP, part, width), bf16),
            pltpu.VMEM((n, CAP, part, width), bf16),
            pltpu.VMEM((n, CAP, part, width), bf16),
            pltpu.VMEM((CHUNKS, owned, part, width), jnp.float32),
            pltpu.VMEM((nv, 8, width), jnp.float32),
            pltpu.VMEM((corr_rows, width), jnp.float32),
            pltpu.VMEM((n, corr_rows, width), jnp.float32),
            pltpu.SMEM((n * CAP,), jnp.int32),
            dma((2,)),
            dma((envs,)),
            dma((envs,)),
            dma((CHUNKS, n)),
            dma((CHUNKS, n)),
            dma((CHUNKS, n)),
            dma((CHUNKS, n)),
            dma((n,)),
            dma((n,)),
        ],
        compiler_params=pltpu.CompilerParams(
            collective_id=0, has_side_effects=True, vmem_limit_bytes=60 * 2**20
        ),
        cost_estimate=pl.CostEstimate(
            flops=flops, bytes_accessed=10 * 2**20, transcendentals=0
        ),
    )(
        source_owner.reshape(-1),
        source_slot,
        target_owner.reshape(-1),
        target_slot,
        wave_blocks,
        davidson_basis,
        left_env,
        right_env,
    )


def solution(mesh):
    return jax.shard_map(
        shards,
        mesh=mesh,
        in_specs=(
            P(("groups", "sector"), None, None),
            P(None, ("groups", "sector"), None, None),
            P(("groups", "sector"), None, None, None),
            P(("groups", "sector"), None, None, None),
            P("groups", None),
            P("groups"),
            P("groups", None),
            P("groups"),
        ),
        out_specs=(P(("groups", "sector"), None, None), P("groups")),
        check_vma=False,
    )
```

time: 145 us -> 67.5 us (0.47)
  waiting for transfers between devices: 76 us -> 0 us
  Pallas kernels: 0 us -> 63.9 us
  blocking collectives: 35.3 us -> 0 us
  between operations: 14.1 us -> 0.64 us
  matrix products: 7.08 us -> 0 us
  local copies, waits for them, and re-layouts: 7.04 us -> 2.8 us
  starting transfers between devices: 3.69 us -> 0 us
  other arithmetic: 1.64 us -> 0 us
    pallas_call x0 -> x1, Pallas kernels: none -> 63.9 us  [shards(): pl.pallas_call(functools.partial(kernel, n, repeats), out_shape=(jax.Shap...]
    all_gather x1 -> x0, waiting for transfers between devices: 53.4 us -> none  [shards(): everything = lax.all_gather(wave_blocks, 'sector', axis=0, tiled=True)]
    psum x1 -> x0, blocking collectives: 35.3 us -> none  [shards(): correlations = lax.psum(partial_value, 'sector')]
    all_to_all x1 -> x0, waiting for transfers between devices: 21.9 us -> none  [shards(): lax.all_to_all(results[back_index], 'sector', split_axis=0, concat_axis=0...]
    dot_general x3 -> x0, matrix products: 7.08 us -> none  [the longest x1 4.6 us: shards(): jnp.einsum('axwl,cwls->acxs', left_env, contracted, preferred_element_typ...]
    gather x2 -> x0, local copies, waits for them, and re-layouts: 4.5 us -> none  [the longest x1 2.83 us: shards(): inputs = everything[my_owners * owned + my_slots]]
    all_to_all x1 -> x0, starting transfers between devices: 3.65 us -> none  [shards(): lax.all_to_all(results[back_index], 'sector', split_axis=0, concat_axis=0...]
    unnamed x7 -> x2, local copies, waits for them, and re-layouts: 0.78 us -> 2.8 us
  transfers between devices with their start and end apart: 2 -> 0, of which waited for: 2 -> 0; matrix products, arithmetic and copies ran while one was open for 2% -> 0% of each run, Pallas kernels for 0% -> 0%
where the time goes in v1:
time: 67.5 us; the launch traced here: 67.3 us
  Pallas kernels  63.9 us (95%)
  local copies, waits for them, and re-layouts  2.8 us (4%)
    pallas_call x1, Pallas kernels, shards(): pl.pallas_call(functools.partial(kernel, n, repeats), out_shape=(jax.Shap...  63.9 us
    unnamed x2, local copies, waits for them, and re-layouts  2.8 us

profile of v1, /device:TPU:0, one launch (start us, length us, event | category | flops | bytes accessed | tf_op | source)
XLA Modules:
  0.0 67.3 jit_solution(14308654759466962359)
XLA Ops:
  0.6 63.9 %shard_map.95 = (bf16[8,128,128]{2,1,0:T(8,128)(2,1)}, f32[4]{0:T(128)}) custom-call(s32[256]{0:T(256)} %bitcast.2, s32[256]{0:T(256)} %sslot.1, s32[256]{0:T(256)} %bitcast.3, s32[256]{0:T(256)} %tslot.1, bf16[8,128,128]{2,1,0:T(8,128)(2,1)} %wave_hbm.1, bf16[4,8,128,128]{3,2,1,0:T(8,128)(2,1)} %dav_hbm.1, bf16[4,128,16,128]{3,2,1,0:T(8,128)(2,1)} %left_hbm.1, ...), custom_call_target="tpu_custom_call" | custom-call | flops 2147483648 | bytes 10485760 | tf_op jit(solution)/shard_map/pallas_call | solution.py:353
  64.5 1.7 %copy.12 = bf16[8,128,128]{2,1,0:T(8,128)(2,1)} copy(bf16[8,128,128]{2,1,0:T(8,128)(2,1)} %get-tuple-element.4) | data formatting | bytes 524288
  66.2 1.1 %copy.13 = f32[4]{0:T(128)} copy(f32[4]{0:T(128)} %get-tuple-element.5) | data formatting | bytes 32

commit v2 on v1

v2 whole, which is shorter than its diff:
```python
import functools

import jax
import jax.numpy as jnp
from jax import lax
from jax.experimental import pallas as pl
from jax.experimental.pallas import tpu as pltpu
from jax.sharding import PartitionSpec as P

CAP = 2
CHUNKS = 2
LINE = 4
MESH = pl.DeviceIdType.MESH


def two_hits(owner_ref, base, rows, who, value, default):
    def step(at, found):
        first, second = found
        row = rows - 1 - at
        hit = owner_ref[base + row] == who
        return jnp.where(hit, value(row), first), jnp.where(hit, first, second)

    start = (jnp.int32(default), jnp.int32(default))
    return lax.fori_loop(0, rows, step, start, unroll=16)


def kernel(
    n,
    repeats,
    sown,
    sslot,
    town,
    tslot,
    wave_hbm,
    dav_hbm,
    left_hbm,
    right_hbm,
    applied_ref,
    corr_ref,
    wave,
    dav,
    raw_r,
    raw_l,
    flat_r,
    flat_l,
    operand,
    contracted,
    acc,
    corr_send,
    corr_recv,
    corr_col,
    corr_lin,
    take,
    rank_of,
    chosen,
    landing,
    load_sem,
    right_sem,
    left_sem,
    raw_ssem,
    raw_rsem,
    col_ssem,
    col_rsem,
    ocol_ssem,
    ocol_rsem,
    line_ssem,
    line_rsem,
    corr_ssem,
    corr_rsem,
    corz_ssem,
    corz_rsem,
    *parts,
):
    me = lax.axis_index("sector")
    side = n // LINE
    z, r = me // side, me % side
    rows = sslot.shape[0] // n
    owned, width = wave.shape[0], wave.shape[1]
    envs = right_hbm.shape[0]
    terms = right_hbm.shape[2]
    nv = dav.shape[0]
    part = width // CHUNKS
    hops = LINE - 1
    grouped = [parts[at * CHUNKS : (at + 1) * CHUNKS] for at in range(len(parts) // CHUNKS)]
    relay = [[grouped[d * hops + k] for k in range(hops)] for d in range(2)]
    col_send, in_recv, res, ocol_send, ocol_recv, line_send, line_recv = grouped[2 * hops :]
    step = (1, -1)

    def has(d, k):
        return z >= k if d == 0 else z + k < LINE

    def next_of(d):
        return jnp.clip(z + step[d], 0, LINE - 1) * side + r

    load_wave = pltpu.make_async_copy(wave_hbm, wave, load_sem.at[0])
    load_dav = pltpu.make_async_copy(dav_hbm, dav, load_sem.at[1])

    def load_right(b):
        return pltpu.make_async_copy(right_hbm.at[b], raw_r.at[b], right_sem.at[b])

    def load_left(a):
        return pltpu.make_async_copy(left_hbm.at[a], raw_l.at[a], left_sem.at[a])

    barrier = pltpu.get_barrier_semaphore()

    for o in range(1, LINE):
        pl.semaphore_signal(
            barrier,
            inc=1,
            device_id={"sector": lax.rem(z + o, LINE) * side + r},
            device_id_type=MESH,
        )

    @pl.loop(1, side)
    def _(o):
        pl.semaphore_signal(
            barrier,
            inc=1,
            device_id={"sector": z * side + lax.rem(r + o, side)},
            device_id_type=MESH,
        )

    load_wave.start()
    for b in range(envs):
        load_right(b).start()
    for a in range(envs):
        load_left(a).start()
    load_dav.start()

    @pl.loop(0, n)
    def _(at):
        s, to = at // side, at % side
        base = (z * side + to) * rows
        hits = two_hits(sown, base, rows, s * side + r, lambda row: sslot[base + row], 0)
        for k in range(CAP):
            take[at * CAP + k] = hits[k]

    load_wave.wait()

    def raw_copy(d, k, q):
        src = wave.at[:, q * part : (q + 1) * part, :] if k == 0 else relay[d][k - 1][q]
        return pltpu.make_async_remote_copy(
            src_ref=src,
            dst_ref=relay[d][k][q],
            send_sem=raw_ssem.at[d, k, q],
            recv_sem=raw_rsem.at[d, k, q],
            device_id={"sector": next_of(d)},
            device_id_type=MESH,
        )

    def col_copy(q, s, to, frm):
        return pltpu.make_async_remote_copy(
            src_ref=col_send[q].at[s, to],
            dst_ref=in_recv[q].at[s * side + frm],
            send_sem=col_ssem.at[q, s, to],
            recv_sem=col_rsem.at[q, s, frm],
            device_id={"sector": z * side + to},
            device_id_type=MESH,
        )

    def hand_out(q, s, load):
        @pl.loop(1, side)
        def _(o):
            to = lax.rem(r + o, side)
            for k in range(CAP):
                col_send[q][s, to, k] = load(take[(s * side + to) * CAP + k])
            col_copy(q, s, to, r).start()

        for k in range(CAP):
            in_recv[q][s * side + r, k] = load(take[(s * side + r) * CAP + k])

    pl.semaphore_wait(barrier, LINE - 1 + side - 1)

    for q in range(CHUNKS):
        for d in range(2):
            ahead = z < LINE - 1 if d == 0 else z > 0

            @pl.when(ahead)
            def _():
                raw_copy(d, 0, q).start()

    for q in range(CHUNKS):
        hand_out(q, z, lambda slot: wave[slot, q * part : (q + 1) * part, :])

    tile = 16
    per_env = width // tile

    def flatten_right(b):
        load_right(b).wait()

        @pl.loop(0, per_env)
        def _(i):
            at = pl.multiple_of(i * tile, tile)
            block = jnp.swapaxes(raw_r[b, pl.ds(at, tile)], 0, 1)
            to = pl.multiple_of(b * width + at, tile)
            for w in range(terms):
                flat_r[pl.ds(to, tile), w * width : (w + 1) * width] = block[w]

    def flatten_left(a):
        load_left(a).wait()

        @pl.loop(0, per_env)
        def _(i):
            x = pl.multiple_of(i * tile, tile)
            block = jnp.swapaxes(raw_l[a, pl.ds(x, tile)], 0, 1)
            to = pl.multiple_of((x // part) * envs * part + a * part + x % part, tile)
            for w in range(terms):
                flat_l[pl.ds(to, tile), w * width : (w + 1) * width] = block[w]

    def ranks():
        @pl.loop(0, rows)
        def _(i):
            owner = sown[me * rows + i]

            def count(h, seen):
                same = (sown[me * rows + h] == owner) & (h < i)
                return seen + same.astype(jnp.int32)

            rank = lax.fori_loop(0, rows, count, jnp.int32(0), unroll=16)
            rank_of[i] = owner * CAP + jnp.minimum(rank, CAP - 1)

    def result_tables():
        @pl.loop(0, n)
        def _(p):
            hits = two_hits(town, me * rows, rows, p, lambda row: row, 0)
            for k in range(CAP):
                chosen[p * CAP + k] = hits[k]

        @pl.loop(0, n)
        def _(at):
            s, frm = at // side, at % side
            base = (z * side + frm) * rows
            hits = two_hits(town, base, rows, s * side + r, lambda row: tslot[base + row], -1)
            for k in range(CAP):
                landing[at * CAP + k] = hits[k]

    chores = [functools.partial(flatten_right, b) for b in range(envs)]
    chores += [functools.partial(flatten_left, a) for a in range(envs)]
    chores += [ranks, result_tables]
    stops = hops * CHUNKS
    stop = 0
    for k in range(hops):
        for q in range(CHUNKS):
            for chore in chores[stop * len(chores) // stops : (stop + 1) * len(chores) // stops]:
                chore()
            stop += 1
            for d in range(2):

                @pl.when(has(d, k + 1))
                def _():
                    raw_copy(d, k, q).wait_recv()
                    if k + 1 < hops:
                        ahead = z < LINE - 1 if d == 0 else z > 0

                        @pl.when(ahead)
                        def _():
                            raw_copy(d, k + 1, q).start()

            for d in range(2):

                @pl.when(has(d, k + 1))
                def _():
                    hand_out(q, z - step[d] * (k + 1), lambda slot: relay[d][k][q][slot])

    for q in range(CHUNKS):

        @pl.loop(0, LINE * (side - 1))
        def _(t):
            frm = lax.rem(r + 1 + t % (side - 1), side)
            col_copy(q, t // (side - 1), frm, frm).wait_recv()

        @pl.loop(0, rows)
        def _(i):
            b = i // repeats
            c = i % repeats
            at = rank_of[i]
            operand[
                pl.ds(pl.multiple_of(c * part, part), part),
                pl.ds(pl.multiple_of(b * width, width), width),
            ] = in_recv[q][at // CAP, at % CAP]

        @pl.loop(0, terms // 2)
        def _(pair):
            cols = pl.ds(pl.multiple_of(pair * 2 * width, 2 * width), 2 * width)
            out = jnp.dot(
                operand[...], flat_r[:, cols], preferred_element_type=jnp.float32
            ).astype(jnp.bfloat16)
            for c in range(repeats):
                for h in range(2):
                    at = pl.multiple_of((pair * 2 + h) * width + q * part, part)
                    contracted[pl.ds(at, part), c * width : (c + 1) * width] = out[
                        c * part : (c + 1) * part, h * width : (h + 1) * width
                    ]

    def ocol_copy(q, s, to, frm):
        return pltpu.make_async_remote_copy(
            src_ref=ocol_send[q].at[s, to],
            dst_ref=ocol_recv[q].at[s, frm],
            send_sem=ocol_ssem.at[q, s, to],
            recv_sem=ocol_rsem.at[q, s, frm],
            device_id={"sector": z * side + to},
            device_id_type=MESH,
        )

    def target(t):
        return jnp.where(z < LINE // 2, LINE - 1 - t, t)

    for q in range(CHUNKS):
        lhs_rows = slice(q * envs * part, (q + 1) * envs * part)

        @pl.loop(0, repeats // 2)
        def _(pair):
            cols = pl.ds(pl.multiple_of(pair * 2 * width, 2 * width), 2 * width)
            out = jnp.dot(
                flat_l[lhs_rows, :], contracted[:, cols], preferred_element_type=jnp.float32
            ).astype(jnp.bfloat16)
            for a in range(envs):
                for h in range(2):
                    res[q][a * repeats + pair * 2 + h] = out[
                        a * part : (a + 1) * part, h * width : (h + 1) * width
                    ]

        @pl.loop(0, LINE)
        def _(t):
            s = target(t)

            @pl.loop(1, side)
            def _(o):
                to = lax.rem(r + o, side)
                for k in range(CAP):
                    ocol_send[q][s, to, k] = res[q][chosen[(s * side + to) * CAP + k]]
                ocol_copy(q, s, to, r).start()

            for k in range(CAP):
                ocol_recv[q][s, r, k] = res[q][chosen[(s * side + r) * CAP + k]]

    def column_sum(q, s):
        @pl.loop(1, side)
        def _(o):
            frm = lax.rem(r + o, side)
            ocol_copy(q, s, frm, frm).wait_recv()

        @pl.loop(0, part // tile)
        def _(i):
            at = pl.ds(pl.multiple_of(i * tile, tile), tile)

            def add(frm, totals):
                totals = list(totals)
                for k in range(CAP):
                    value = ocol_recv[q][s, frm, k, at].astype(jnp.float32)
                    land = landing[(s * side + frm) * CAP + k]
                    for b in range(owned):
                        totals[b] = totals[b] + jnp.where(land == b, 1.0, 0.0) * value
                return tuple(totals)

            zero = tuple(jnp.zeros((tile, width), jnp.float32) for _ in range(owned))
            totals = lax.fori_loop(0, side, add, zero, unroll=4)
            for b in range(owned):
                acc[b, at] = totals[b]

    def line_copy(d, k, q):
        return pltpu.make_async_remote_copy(
            src_ref=line_send[q].at[d, k],
            dst_ref=line_recv[q].at[d, k],
            send_sem=line_ssem.at[d, k, q],
            recv_sem=line_rsem.at[d, k, q],
            device_id={"sector": next_of(d)},
            device_id_type=MESH,
        )

    def add_line(d, k, q):
        line_copy(d, k, q).wait_recv()

        @pl.loop(0, owned)
        def _(b):
            acc[b] = acc[b] + line_recv[q][d, k, b].astype(jnp.float32)

    for k in reversed(range(hops)):
        for q in range(CHUNKS):
            for d in range(2):
                exists = z + k + 1 < LINE if d == 0 else z >= k + 1

                @pl.when(exists)
                def _():
                    column_sum(q, z + step[d] * (k + 1))
                    if k + 1 < hops:

                        @pl.when(has(d, 1))
                        def _():
                            add_line(d, k + 1, q)

                    @pl.loop(0, owned)
                    def _(b):
                        line_send[q][d, k, b] = acc[b].astype(jnp.bfloat16)

                    line_copy(d, k, q).start()

    load_dav.wait()
    partial = [jnp.zeros((8, width), jnp.float32) for _ in range(nv)]
    for q in range(CHUNKS):
        column_sum(q, z)
        for d in range(2):

            @pl.when(has(d, 1))
            def _():
                add_line(d, 0, q)

        for b in range(owned):
            block = acc[b].astype(jnp.bfloat16)
            applied_ref[b, q * part : (q + 1) * part, :] = block
            block = block.astype(jnp.float32)
            for v in range(nv):
                prod = dav[v, b, q * part : (q + 1) * part, :].astype(jnp.float32) * block
                partial[v] = partial[v] + jnp.sum(prod.reshape(part // 8, 8, width), axis=0)

    for v in range(nv):
        corr_send[v : v + 1, :] = jnp.sum(partial[v], axis=0, keepdims=True)
    if nv < corr_send.shape[0]:
        corr_send[nv:, :] = jnp.zeros((corr_send.shape[0] - nv, width), jnp.float32)

    def corr_copy(to, frm):
        return pltpu.make_async_remote_copy(
            src_ref=corr_send,
            dst_ref=corr_recv.at[frm],
            send_sem=corr_ssem.at[to],
            recv_sem=corr_rsem.at[frm],
            device_id={"sector": z * side + to},
            device_id_type=MESH,
        )

    def corz_copy(to, frm):
        return pltpu.make_async_remote_copy(
            src_ref=corr_col,
            dst_ref=corr_lin.at[frm],
            send_sem=corz_ssem.at[to],
            recv_sem=corz_rsem.at[frm],
            device_id={"sector": to * side + r},
            device_id_type=MESH,
        )

    @pl.loop(1, side)
    def _(o):
        corr_copy(lax.rem(r + o, side), r).start()

    corr_recv[r] = corr_send[...]

    for q in range(CHUNKS):

        @pl.loop(0, LINE * (side - 1))
        def _(t):
            to = lax.rem(r + 1 + t % (side - 1), side)
            col_copy(q, t // (side - 1), to, r).wait_send()
            ocol_copy(q, t // (side - 1), to, r).wait_send()

        for d in range(2):
            for k in range(hops):
                ahead = z < LINE - 1 if d == 0 else z > 0

                @pl.when(ahead & has(d, k))
                def _():
                    raw_copy(d, k, q).wait_send()

                exists = z + k + 1 < LINE if d == 0 else z >= k + 1

                @pl.when(exists)
                def _():
                    line_copy(d, k, q).wait_send()

    @pl.loop(1, side)
    def _(o):
        frm = lax.rem(r + o, side)
        corr_copy(frm, frm).wait_recv()

    corr_col[...] = jnp.sum(corr_recv[...], axis=0)
    for o in range(1, LINE):
        corz_copy(lax.rem(z + o, LINE), z).start()
    corr_lin[z] = corr_col[...]

    @pl.loop(1, side)
    def _(o):
        corr_copy(lax.rem(r + o, side), r).wait_send()

    for o in range(1, LINE):
        frm = lax.rem(z + o, LINE)
        corz_copy(frm, frm).wait_recv()

    total = jnp.sum(corr_lin[...], axis=0)
    for v in range(nv):
        corr_ref[v] = jnp.sum(total[v : v + 1, :])

    for o in range(1, LINE):
        corz_copy(lax.rem(z + o, LINE), z).wait_send()


def shards(
    wave_blocks,
    davidson_basis,
    left_env,
    right_env,
    source_owner,
    source_slot,
    target_owner,
    target_slot,
):
    n = lax.axis_size("sector")
    owned, width = wave_blocks.shape[0], wave_blocks.shape[1]
    envs, terms = right_env.shape[0], right_env.shape[2]
    rows = source_slot.shape[0] // n
    repeats = rows // envs
    nv = davidson_basis.shape[0]
    part = width // CHUNKS
    side, hops = n // LINE, LINE - 1
    corr_rows = -(-nv // 8) * 8
    bf16 = jnp.bfloat16
    smem = pl.BlockSpec(memory_space=pltpu.SMEM)
    vmem = pl.BlockSpec(memory_space=pltpu.VMEM)
    hbm = pl.BlockSpec(memory_space=pl.ANY)
    dma = pltpu.SemaphoreType.DMA
    flops = 4 * rows * terms * width**3
    return pl.pallas_call(
        functools.partial(kernel, n, repeats),
        out_shape=(
            jax.ShapeDtypeStruct((owned, width, width), bf16),
            jax.ShapeDtypeStruct((nv,), jnp.float32),
        ),
        in_specs=[smem] * 4 + [hbm] * 4,
        out_specs=(vmem, smem),
        scratch_shapes=[
            pltpu.VMEM((owned, width, width), bf16),
            pltpu.VMEM((nv, owned, width, width), bf16),
            pltpu.VMEM((envs, width, terms, width), bf16),
            pltpu.VMEM((envs, width, terms, width), bf16),
            pltpu.VMEM((envs * width, terms * width), bf16),
            pltpu.VMEM((envs * width, terms * width), bf16),
            pltpu.VMEM((repeats * part, envs * width), bf16),
            pltpu.VMEM((terms * width, repeats * width), bf16),
            pltpu.VMEM((owned, part, width), jnp.float32),
            pltpu.VMEM((corr_rows, width), jnp.float32),
            pltpu.VMEM((side, corr_rows, width), jnp.float32),
            pltpu.VMEM((corr_rows, width), jnp.float32),
            pltpu.VMEM((LINE, corr_rows, width), jnp.float32),
            pltpu.SMEM((n * CAP,), jnp.int32),
            pltpu.SMEM((rows,), jnp.int32),
            pltpu.SMEM((n * CAP,), jnp.int32),
            pltpu.SMEM((n * CAP,), jnp.int32),
            dma((2,)),
            dma((envs,)),
            dma((envs,)),
            dma((2, hops, CHUNKS)),
            dma((2, hops, CHUNKS)),
            dma((CHUNKS, LINE, side)),
            dma((CHUNKS, LINE, side)),
            dma((CHUNKS, LINE, side)),
            dma((CHUNKS, LINE, side)),
            dma((2, hops, CHUNKS)),
            dma((2, hops, CHUNKS)),
            dma((side,)),
            dma((side,)),
            dma((LINE,)),
            dma((LINE,)),
        ]
        + [pltpu.VMEM((owned, part, width), bf16)] * (2 * hops * CHUNKS)
        + [pltpu.VMEM((LINE, side, CAP, part, width), bf16)] * CHUNKS
        + [pltpu.VMEM((n, CAP, part, width), bf16)] * CHUNKS
        + [pltpu.VMEM((rows, part, width), bf16)] * CHUNKS
        + [pltpu.VMEM((LINE, side, CAP, part, width), bf16)] * (2 * CHUNKS)
        + [pltpu.VMEM((2, hops, owned, part, width), bf16)] * (2 * CHUNKS),
        compiler_params=pltpu.CompilerParams(
            collective_id=0, has_side_effects=True, vmem_limit_bytes=60 * 2**20
        ),
        cost_estimate=pl.CostEstimate(
            flops=flops, bytes_accessed=10 * 2**20, transcendentals=0
        ),
    )(
        source_owner.reshape(-1),
        source_slot,
        target_owner.reshape(-1),
        target_slot,
        wave_blocks,
        davidson_basis,
        left_env,
        right_env,
    )


def solution(mesh):
    return jax.shard_map(
        shards,
        mesh=mesh,
        in_specs=(
            P(("groups", "sector"), None, None),
            P(None, ("groups", "sector"), None, None),
            P(("groups", "sector"), None, None, None),
            P(("groups", "sector"), None, None, None),
            P("groups", None),
            P("groups"),
            P("groups", None),
            P("groups"),
        ),
        out_specs=(P(("groups", "sector"), None, None), P("groups")),
        check_vma=False,
    )
```

time: 67.5 us -> 69.1 us (1.024)
  Pallas kernels: 63.9 us -> 65.5 us
    pallas_call x1, Pallas kernels: 63.9 us -> 65.5 us  [shards(): pl.pallas_call(functools.partial(kernel, n, repeats), out_shape=(jax.Shap...]
where the time goes in v2:
time: 69.1 us; the launch traced here: 68.9 us
  Pallas kernels  65.5 us (95%)
  local copies, waits for them, and re-layouts  2.8 us (4%)
    pallas_call x1, Pallas kernels, shards(): pl.pallas_call(functools.partial(kernel, n, repeats), out_shape=(jax.Shap...  65.5 us
    unnamed x2, local copies, waits for them, and re-layouts  2.8 us

profile of v2, /device:TPU:0, one launch (start us, length us, event | category | flops | bytes accessed | tf_op | source)
XLA Modules:
  0.0 68.9 jit_solution(6658779224106406522)
XLA Ops:
  0.6 65.5 %shard_map.95 = (bf16[8,128,128]{2,1,0:T(8,128)(2,1)}, f32[4]{0:T(128)}) custom-call(s32[256]{0:T(256)} %bitcast.2, s32[256]{0:T(256)} %sslot.1, s32[256]{0:T(256)} %bitcast.3, s32[256]{0:T(256)} %tslot.1, bf16[8,128,128]{2,1,0:T(8,128)(2,1)} %wave_hbm.1, bf16[4,8,128,128]{3,2,1,0:T(8,128)(2,1)} %dav_hbm.1, bf16[4,128,16,128]{3,2,1,0:T(8,128)(2,1)} %left_hbm.1, ...), custom_call_target="tpu_custom_call" | custom-call | flops 2147483648 | bytes 10485760 | tf_op jit(solution)/shard_map/pallas_call | solution.py:520
  66.1 1.7 %copy.12 = bf16[8,128,128]{2,1,0:T(8,128)(2,1)} copy(bf16[8,128,128]{2,1,0:T(8,128)(2,1)} %get-tuple-element.4) | data formatting | bytes 524288
  67.8 1.1 %copy.13 = f32[4]{0:T(128)} copy(f32[4]{0:T(128)} %get-tuple-element.5) | data formatting | bytes 32

commit v3 on v1

--- a/solution.py
+++ b/solution.py
@@ -59,6 +59,17 @@
     corr_send,
     corr_recv,
     landing,
+    take,
+    take_far,
+    rank_of,
+    chosen,
+    raw0,
+    raw1,
+    far_send0,
+    far_send1,
+    raw_ssem,
+    raw_rsem,
+    far_ssem,
     load_sem,
     right_sem,
     left_sem,
@@ -76,6 +87,11 @@
     terms = right_hbm.shape[2]
     nv = dav.shape[0]
     part = width // CHUNKS
+    half = n // 2
+    mine = me // half
+    inner = ((me // (half // 2)) % 3) != 0
+    partner = lax.rem(me + half, n)
+    raw, far_send = (raw0, raw1), (far_send0, far_send1)
     in_send, in_recv = (in_send0, in_send1), (in_recv0, in_recv1)
     res = (res0, res1)
     out_send, out_recv = (out_send0, out_send1), (out_recv0, out_recv1)
@@ -96,6 +112,14 @@
 
     def load_left(a):
         return pltpu.make_async_copy(left_hbm.at[a], raw_l.at[a], left_sem.at[a])
+
+    barrier = pltpu.get_barrier_semaphore()
+
+    @pl.loop(0, n - 1)
+    def _(t):
+        pl.semaphore_signal(
+            barrier, inc=1, device_id={"sector": peer(t)}, device_id_type=MESH
+        )
 
     load_wave.start()
     for b in range(envs):
@@ -104,25 +128,28 @@
         load_left(a).start()
     load_dav.start()
 
-    barrier = pltpu.get_barrier_semaphore()
+    def pick(p, owner):
+        return two_hits(sown, p * rows, rows, owner, lambda row: sslot[p * rows + row], 0)
+
+    @pl.loop(0, n)
+    def _(p):
+        for k, slot in enumerate(pick(p, me)):
+            take[p * CAP + k] = slot
+
+    load_wave.wait()
+
+    for k in range(CAP):
+        slot = take[me * CAP + k]
+        for q in range(CHUNKS):
+            in_recv[q][me, k] = wave[slot, q * part : (q + 1) * part, :]
 
     @pl.loop(0, n - 1)
     def _(t):
-        pl.semaphore_signal(
-            barrier, inc=1, device_id={"sector": peer(t)}, device_id_type=MESH
-        )
-
-    load_wave.wait()
-
-    def pick(p):
-        return two_hits(sown, p * rows, rows, me, lambda row: sslot[p * rows + row], 0)
-
-    own0, own1 = pick(me)
-    for k, slot in enumerate((own0, own1)):
-        for q in range(CHUNKS):
-            in_recv[q][me, k] = wave[slot, q * part : (q + 1) * part, :]
-
-    pl.semaphore_wait(barrier, n - 1)
+        p = peer(t)
+        for k in range(CAP):
+            slot = take[p * CAP + k]
+            for q in range(CHUNKS):
+                in_send[q][p, k] = wave[slot, q * part : (q + 1) * part, :]
 
     def in_copy(q, to, frm):
         return pltpu.make_async_remote_copy(
@@ -134,18 +161,67 @@
             device_id_type=MESH,
         )
 
-    @pl.loop(0, n - 1)
-    def _(t):
-        p = peer(t)
-        slots = pick(p)
-        for k in range(CAP):
-            for q in range(CHUNKS):
-                in_send[q][p, k] = wave[slots[k], q * part : (q + 1) * part, :]
-        in_copy(0, p, me).start()
-
-    @pl.loop(0, n - 1)
-    def _(t):
-        in_copy(1, peer(t), me).start()
+    def raw_copy(q):
+        return pltpu.make_async_remote_copy(
+            src_ref=wave.at[:, q * part : (q + 1) * part, :],
+            dst_ref=raw[q],
+            send_sem=raw_ssem.at[q],
+            recv_sem=raw_rsem.at[q],
+            device_id={"sector": partner},
+            device_id_type=MESH,
+        )
+
+    def far_copy(q, to):
+        return pltpu.make_async_remote_copy(
+            src_ref=far_send[q].at[to % half],
+            dst_ref=in_recv[q].at[partner],
+            send_sem=far_ssem.at[q, to % half],
+            recv_sem=in_rsem.at[q, partner],
+            device_id={"sector": to},
+            device_id_type=MESH,
+        )
+
+    def direct(p):
+        return inner | (p // half == mine)
+
+    def nearby(o):
+        return mine * half + lax.rem(me % half + o, half)
+
+    pl.semaphore_wait(barrier, n - 1)
+
+    for q in range(CHUNKS):
+
+        @pl.when(jnp.logical_not(inner))
+        def _():
+            raw_copy(q).start()
+
+        @pl.loop(0, n - 1)
+        def _(t):
+            p = peer(t)
+
+            @pl.when(direct(p))
+            def _():
+                in_copy(q, p, me).start()
+
+    @pl.loop(0, n)
+    def _(p):
+        for k, slot in enumerate(pick(p, partner)):
+            take_far[p * CAP + k] = slot
+
+    def hand_on(q):
+        @pl.when(inner)
+        def _():
+            raw_copy(q).wait_recv()
+
+            @pl.loop(1, half)
+            def _(o):
+                p = nearby(o)
+                for k in range(CAP):
+                    far_send[q][p % half, k] = raw[q][take_far[p * CAP + k]]
+                far_copy(q, p).start()
+
+            for k in range(CAP):
+                in_recv[q][partner, k] = raw[q][take_far[me * CAP + k]]
 
     tile = 16
     for b in range(envs):
@@ -159,6 +235,8 @@
         block = jnp.swapaxes(raw_r[b, pl.ds(r, tile)], 0, 1)
         for w in range(terms):
             flat_r[pl.ds(pl.multiple_of(b * width + r, tile), tile), w * width : (w + 1) * width] = block[w]
+
+    hand_on(0)
 
     for a in range(envs):
         load_left(a).wait()
@@ -180,30 +258,46 @@
         for k in range(CAP):
             landing[j * CAP + k] = hits[k]
 
+    hand_on(1)
     acc[...] = jnp.zeros_like(acc)
     load_dav.wait()
 
+    @pl.loop(0, rows)
+    def _(i):
+        owner = sown[me * rows + i]
+
+        def count(h, seen):
+            same = (sown[me * rows + h] == owner) & (h < i)
+            return seen + same.astype(jnp.int32)
+
+        rank = lax.fori_loop(0, rows, count, jnp.int32(0), unroll=16)
+        rank_of[i] = owner * CAP + jnp.minimum(rank, CAP - 1)
+
+    @pl.loop(0, n)
+    def _(p):
+        hits = two_hits(town, me * rows, rows, p, lambda row: row, 0)
+        for k in range(CAP):
+            chosen[p * CAP + k] = hits[k]
+
     for q in range(CHUNKS):
 
         @pl.loop(0, n - 1)
         def _(t):
-            in_copy(q, source(t), source(t)).wait_recv()
+            owner = source(t)
+
+            @pl.when(jnp.logical_not(inner & (owner == partner)))
+            def _():
+                in_copy(q, owner, owner).wait_recv()
 
         @pl.loop(0, rows)
         def _(i):
-            owner = sown[me * rows + i]
-
-            def count(h, seen):
-                same = (sown[me * rows + h] == owner) & (h < i)
-                return seen + same.astype(jnp.int32)
-
-            rank = lax.fori_loop(0, rows, count, jnp.int32(0), unroll=16)
+            at = rank_of[i]
             b = i // repeats
             c = i % repeats
             operand[
                 pl.ds(pl.multiple_of(c * part, part), part),
                 pl.ds(pl.multiple_of(b * width, width), width),
-            ] = in_recv[q][owner, jnp.minimum(rank, CAP - 1)]
+            ] = in_recv[q][at // CAP, at % CAP]
 
         @pl.loop(0, terms // 2)
         def _(pair):
@@ -243,20 +337,15 @@
                         a * part : (a + 1) * part, h * width : (h + 1) * width
                     ]
 
-        def choose(p):
-            return two_hits(town, me * rows, rows, p, lambda row: row, 0)
-
         @pl.loop(0, n - 1)
         def _(t):
             p = peer(t)
-            picked = choose(p)
             for k in range(CAP):
-                out_send[q][p, k] = res[q][picked[k]]
+                out_send[q][p, k] = res[q][chosen[p * CAP + k]]
             out_copy(q, p, me).start()
 
-        picked = choose(me)
         for k in range(CAP):
-            out_recv[q][me, k] = res[q][picked[k]]
+            out_recv[q][me, k] = res[q][chosen[me * CAP + k]]
 
     def add(q, j):
         values = [out_recv[q][j, k].astype(jnp.float32) for k in range(CAP)]
@@ -310,8 +399,23 @@
     def _(t):
         p = peer(t)
         for q in range(CHUNKS):
-            in_copy(q, p, me).wait_send()
             out_copy(q, p, me).wait_send()
+
+            @pl.when(direct(p))
+            def _():
+                in_copy(q, p, me).wait_send()
+
+    for q in range(CHUNKS):
+
+        @pl.when(jnp.logical_not(inner))
+        def _():
+            raw_copy(q).wait_send()
+
+        @pl.when(inner)
+        def _():
+            @pl.loop(1, half)
+            def _(o):
+                far_copy(q, nearby(o)).wait_send()
 
     @pl.loop(0, n - 1)
     def _(t):
@@ -382,6 +486,17 @@
             pltpu.VMEM((corr_rows, width), jnp.float32),
             pltpu.VMEM((n, corr_rows, width), jnp.float32),
             pltpu.SMEM((n * CAP,), jnp.int32),
+            pltpu.SMEM((n * CAP,), jnp.int32),
+            pltpu.SMEM((n * CAP,), jnp.int32),
+            pltpu.SMEM((rows,), jnp.int32),
+            pltpu.SMEM((n * CAP,), jnp.int32),
+            pltpu.VMEM((owned, part, width), bf16),
+            pltpu.VMEM((owned, part, width), bf16),
+            pltpu.VMEM((n // 2, CAP, part, width), bf16),
+            pltpu.VMEM((n // 2, CAP, part, width), bf16),
+            dma((CHUNKS,)),
+            dma((CHUNKS,)),
+            dma((CHUNKS, n // 2)),
             dma((2,)),
             dma((envs,)),
             dma((envs,)),

time: 67.5 us -> 63.1 us (0.935)
  Pallas kernels: 63.9 us -> 59.5 us
    pallas_call x1, Pallas kernels: 63.9 us -> 59.5 us  [shards(): pl.pallas_call(functools.partial(kernel, n, repeats), out_shape=(jax.Shap...]
where the time goes in v3:
time: 63.1 us; the launch traced here: 63 us
  Pallas kernels  59.5 us (94%)
  local copies, waits for them, and re-layouts  2.8 us (4%)
  between operations  0.64 us (1%)
    pallas_call x1, Pallas kernels, shards(): pl.pallas_call(functools.partial(kernel, n, repeats), out_shape=(jax.Shap...  59.5 us
    unnamed x2, local copies, waits for them, and re-layouts  2.8 us

profile of v3, /device:TPU:0, one launch (start us, length us, event | category | flops | bytes accessed | tf_op | source)
XLA Modules:
  0.0 63.0 jit_solution(362268146099526357)
XLA Ops:
  0.6 59.5 %shard_map.95 = (bf16[8,128,128]{2,1,0:T(8,128)(2,1)}, f32[4]{0:T(128)}) custom-call(s32[256]{0:T(256)} %bitcast.2, s32[256]{0:T(256)} %sslot.1, s32[256]{0:T(256)} %bitcast.3, s32[256]{0:T(256)} %tslot.1, bf16[8,128,128]{2,1,0:T(8,128)(2,1)} %wave_hbm.1, bf16[4,8,128,128]{3,2,1,0:T(8,128)(2,1)} %dav_hbm.1, bf16[4,128,16,128]{3,2,1,0:T(8,128)(2,1)} %left_hbm.1, ...), custom_call_target="tpu_custom_call" | custom-call | flops 2147483648 | bytes 10485760 | tf_op jit(solution)/shard_map/pallas_call | solution.py:457
  60.2 1.7 %copy.12 = bf16[8,128,128]{2,1,0:T(8,128)(2,1)} copy(bf16[8,128,128]{2,1,0:T(8,128)(2,1)} %get-tuple-element.4) | data formatting | bytes 524288
  61.8 1.1 %copy.13 = f32[4]{0:T(128)} copy(f32[4]{0:T(128)} %get-tuple-element.5) | data formatting | bytes 32

commit v4 on v3

--- a/solution.py
+++ b/solution.py
@@ -70,6 +70,16 @@
     raw_ssem,
     raw_rsem,
     far_ssem,
+    gath0,
+    gath1,
+    sum_send0,
+    sum_send1,
+    sum_recv0,
+    sum_recv1,
+    landing_far,
+    gath_rsem,
+    sum_ssem,
+    sum_rsem,
     load_sem,
     right_sem,
     left_sem,
@@ -91,6 +101,7 @@
     mine = me // half
     inner = ((me // (half // 2)) % 3) != 0
     partner = lax.rem(me + half, n)
+    gath, sum_send, sum_recv = (gath0, gath1), (sum_send0, sum_send1), (sum_recv0, sum_recv1)
     raw, far_send = (raw0, raw1), (far_send0, far_send1)
     in_send, in_recv = (in_send0, in_send1), (in_recv0, in_recv1)
     res = (res0, res1)
@@ -257,6 +268,13 @@
         hits = two_hits(town, j * rows, rows, me, lambda row: tslot[j * rows + row], -1)
         for k in range(CAP):
             landing[j * CAP + k] = hits[k]
+
+    @pl.loop(0, half)
+    def _(h):
+        base = (mine * half + h) * rows
+        hits = two_hits(town, base, rows, partner, lambda row: tslot[base + row], -1)
+        for k in range(CAP):
+            landing_far[h * CAP + k] = hits[k]
 
     hand_on(1)
     acc[...] = jnp.zeros_like(acc)
@@ -322,6 +340,32 @@
             device_id_type=MESH,
         )
 
+    def gather_copy(q, p, to, frm):
+        return pltpu.make_async_remote_copy(
+            src_ref=out_send[q].at[p],
+            dst_ref=gath[q].at[frm],
+            send_sem=out_ssem.at[q, p],
+            recv_sem=gath_rsem.at[q, frm],
+            device_id={"sector": to},
+            device_id_type=MESH,
+        )
+
+    def sum_copy(q):
+        return pltpu.make_async_remote_copy(
+            src_ref=sum_send[q],
+            dst_ref=sum_recv[q],
+            send_sem=sum_ssem.at[q],
+            recv_sem=sum_rsem.at[q],
+            device_id={"sector": partner},
+            device_id_type=MESH,
+        )
+
+    quarter = half // 2
+    far_end = jnp.where(mine == 0, 3, 0) * quarter
+
+    def reached(p):
+        return (p // half == mine) | ((p // quarter) % 3 != 0)
+
     for q in range(CHUNKS):
         lhs_rows = slice(q * envs * part, (q + 1) * envs * part)
 
@@ -337,15 +381,64 @@
                         a * part : (a + 1) * part, h * width : (h + 1) * width
                     ]
 
+        @pl.loop(0, quarter)
+        def _(i):
+            p = far_end + i
+            to = lax.rem(p + half, n)
+            for k in range(CAP):
+                out_send[q][p, k] = res[q][chosen[p * CAP + k]]
+
+            @pl.when(to != me)
+            def _():
+                gather_copy(q, p, to, me % half).start()
+
+        @pl.when(inner)
+        def _():
+            for k in range(CAP):
+                gath[q][me % half, k] = res[q][chosen[partner * CAP + k]]
+
         @pl.loop(0, n - 1)
         def _(t):
             p = peer(t)
-            for k in range(CAP):
-                out_send[q][p, k] = res[q][chosen[p * CAP + k]]
-            out_copy(q, p, me).start()
+
+            @pl.when(reached(p))
+            def _():
+                for k in range(CAP):
+                    out_send[q][p, k] = res[q][chosen[p * CAP + k]]
+                out_copy(q, p, me).start()
 
         for k in range(CAP):
             out_recv[q][me, k] = res[q][chosen[me * CAP + k]]
+
+    tile = 16
+    for q in range(CHUNKS):
+
+        @pl.when(inner)
+        def _():
+            @pl.loop(1, half)
+            def _(o):
+                frm = lax.rem(me % half + o, half)
+                gather_copy(q, partner, me, frm).wait_recv()
+
+            @pl.loop(0, part // tile)
+            def _(i):
+                at = pl.ds(pl.multiple_of(i * tile, tile), tile)
+
+                def gather(frm, totals):
+                    totals = list(totals)
+                    for k in range(CAP):
+                        value = gath[q][frm, k, at].astype(jnp.float32)
+                        land = landing_far[frm * CAP + k]
+                        for b in range(owned):
+                            totals[b] = totals[b] + jnp.where(land == b, 1.0, 0.0) * value
+                    return tuple(totals)
+
+                zero = tuple(jnp.zeros((tile, width), jnp.float32) for _ in range(owned))
+                totals = lax.fori_loop(0, half, gather, zero, unroll=4)
+                for b in range(owned):
+                    sum_send[q][b, at] = totals[b].astype(jnp.bfloat16)
+
+            sum_copy(q).start()
 
     def add(q, j):
         values = [out_recv[q][j, k].astype(jnp.float32) for k in range(CAP)]
@@ -363,8 +456,19 @@
         @pl.loop(0, n - 1)
         def _(t):
             j = source(t)
-            out_copy(q, j, j).wait_recv()
-            add(q, j)
+
+            @pl.when(direct(j))
+            def _():
+                out_copy(q, j, j).wait_recv()
+                add(q, j)
+
+        @pl.when(jnp.logical_not(inner))
+        def _():
+            sum_copy(q).wait_recv()
+
+            @pl.loop(0, owned)
+            def _(d):
+                acc[q, d] = acc[q, d] + sum_recv[q][d].astype(jnp.float32)
 
         for d in range(owned):
             block = acc[q, d].astype(jnp.bfloat16)
@@ -399,7 +503,10 @@
     def _(t):
         p = peer(t)
         for q in range(CHUNKS):
-            out_copy(q, p, me).wait_send()
+
+            @pl.when(reached(p) | (lax.rem(p + half, n) != me))
+            def _():
+                out_copy(q, p, me).wait_send()
 
             @pl.when(direct(p))
             def _():
@@ -410,6 +517,10 @@
         @pl.when(jnp.logical_not(inner))
         def _():
             raw_copy(q).wait_send()
+
+        @pl.when(inner)
+        def _():
+            sum_copy(q).wait_send()
 
         @pl.when(inner)
         def _():
@@ -497,6 +608,16 @@
             dma((CHUNKS,)),
             dma((CHUNKS,)),
             dma((CHUNKS, n // 2)),
+            pltpu.VMEM((n // 2, CAP, part, width), bf16),
+            pltpu.VMEM((n // 2, CAP, part, width), bf16),
+            pltpu.VMEM((owned, part, width), bf16),
+            pltpu.VMEM((owned, part, width), bf16),
+            pltpu.VMEM((owned, part, width), bf16),
+            pltpu.VMEM((owned, part, width), bf16),
+            pltpu.SMEM((n // 2 * CAP,), jnp.int32),
+            dma((CHUNKS, n // 2)),
+            dma((CHUNKS,)),
+            dma((CHUNKS,)),
             dma((2,)),
             dma((envs,)),
             dma((envs,)),

time: 63.1 us -> 59.8 us (0.948)
  Pallas kernels: 59.5 us -> 56.1 us
    pallas_call x1, Pallas kernels: 59.5 us -> 56.1 us  [shards(): pl.pallas_call(functools.partial(kernel, n, repeats), out_shape=(jax.Shap...]
where the time goes in v4:
time: 59.8 us; the launch traced here: 59.6 us
  Pallas kernels  56.1 us (94%)
  local copies, waits for them, and re-layouts  2.8 us (5%)
  between operations  0.64 us (1%)
    pallas_call x1, Pallas kernels, shards(): pl.pallas_call(functools.partial(kernel, n, repeats), out_shape=(jax.Shap...  56.1 us
    unnamed x2, local copies, waits for them, and re-layouts  2.8 us

profile of v4, /device:TPU:0, one launch (start us, length us, event | category | flops | bytes accessed | tf_op | source)
XLA Modules:
  0.0 59.6 jit_solution(9787038300714535276)
XLA Ops:
  0.6 56.1 %shard_map.95 = (bf16[8,128,128]{2,1,0:T(8,128)(2,1)}, f32[4]{0:T(128)}) custom-call(s32[256]{0:T(256)} %bitcast.2, s32[256]{0:T(256)} %sslot.1, s32[256]{0:T(256)} %bitcast.3, s32[256]{0:T(256)} %tslot.1, bf16[8,128,128]{2,1,0:T(8,128)(2,1)} %wave_hbm.1, bf16[4,8,128,128]{3,2,1,0:T(8,128)(2,1)} %dav_hbm.1, bf16[4,128,16,128]{3,2,1,0:T(8,128)(2,1)} %left_hbm.1, ...), custom_call_target="tpu_custom_call" | custom-call | flops 2147483648 | bytes 10485760 | tf_op jit(solution)/shard_map/pallas_call | solution.py:568
  56.8 1.7 %copy.12 = bf16[8,128,128]{2,1,0:T(8,128)(2,1)} copy(bf16[8,128,128]{2,1,0:T(8,128)(2,1)} %get-tuple-element.4) | data formatting | bytes 524288
  58.5 1.1 %copy.13 = f32[4]{0:T(128)} copy(f32[4]{0:T(128)} %get-tuple-element.5) | data formatting | bytes 32

commit v5 on v4

--- a/solution.py
+++ b/solution.py
@@ -26,16 +26,23 @@
 def kernel(
     n,
     repeats,
+    sown_hbm,
+    sslot_hbm,
+    town_hbm,
+    tslot_hbm,
+    wave_hbm,
+    dav_hbm,
+    left_hbm,
+    right_hbm,
+    applied_hbm,
+    corr_ref,
     sown,
     sslot,
     town,
     tslot,
-    wave_hbm,
-    dav_hbm,
-    left_hbm,
-    right_hbm,
     applied_ref,
-    corr_ref,
+    table_sem,
+    store_sem,
     wave,
     dav,
     raw_r,
@@ -132,6 +139,14 @@
             barrier, inc=1, device_id={"sector": peer(t)}, device_id_type=MESH
         )
 
+    tables = [
+        pltpu.make_async_copy(src, dst, table_sem.at[at])
+        for at, (src, dst) in enumerate(
+            ((sown_hbm, sown), (sslot_hbm, sslot), (town_hbm, town), (tslot_hbm, tslot))
+        )
+    ]
+    for table in tables:
+        table.start()
     load_wave.start()
     for b in range(envs):
         load_right(b).start()
@@ -141,6 +156,9 @@
 
     def pick(p, owner):
         return two_hits(sown, p * rows, rows, owner, lambda row: sslot[p * rows + row], 0)
+
+    for table in tables:
+        table.wait()
 
     @pl.loop(0, n)
     def _(p):
@@ -497,6 +515,9 @@
     def _(t):
         corr_copy(peer(t), me).start()
 
+    store = pltpu.make_async_copy(applied_ref, applied_hbm, store_sem)
+    store.start()
+
     corr_recv[me] = corr_send[...]
 
     @pl.loop(0, n - 1)
@@ -532,6 +553,7 @@
     def _(t):
         corr_copy(source(t), source(t)).wait_recv()
 
+    store.wait()
     total = jnp.sum(corr_recv[...], axis=0)
     for v in range(nv):
         corr_ref[v] = jnp.sum(total[v : v + 1, :])
@@ -561,7 +583,6 @@
     corr_rows = -(-nv // 8) * 8
     bf16 = jnp.bfloat16
     smem = pl.BlockSpec(memory_space=pltpu.SMEM)
-    vmem = pl.BlockSpec(memory_space=pltpu.VMEM)
     hbm = pl.BlockSpec(memory_space=pl.ANY)
     dma = pltpu.SemaphoreType.DMA
     flops = 4 * rows * terms * width**3
@@ -571,9 +592,16 @@
             jax.ShapeDtypeStruct((owned, width, width), bf16),
             jax.ShapeDtypeStruct((nv,), jnp.float32),
         ),
-        in_specs=[smem] * 4 + [hbm] * 4,
-        out_specs=(vmem, smem),
+        in_specs=[hbm] * 8,
+        out_specs=(hbm, smem),
         scratch_shapes=[
+            pltpu.SMEM((rows * n,), jnp.int32),
+            pltpu.SMEM((rows * n,), jnp.int32),
+            pltpu.SMEM((rows * n,), jnp.int32),
+            pltpu.SMEM((rows * n,), jnp.int32),
+            pltpu.VMEM((owned, width, width), bf16),
+            dma((4,)),
+            dma,
             pltpu.VMEM((owned, width, width), bf16),
             pltpu.VMEM((nv, owned, width, width), bf16),
             pltpu.VMEM((envs, width, terms, width), bf16),

time: 59.8 us -> 58.9 us (0.985)
  Pallas kernels: 56.1 us -> 55.2 us
    pallas_call x1, Pallas kernels: 56.1 us -> 55.2 us  [shards(): pl.pallas_call(functools.partial(kernel, n, repeats), out_shape=(jax.Shap...]
where the time goes in v5:
time: 58.9 us; the launch traced here: 58.7 us
  Pallas kernels  55.2 us (94%)
  local copies, waits for them, and re-layouts  2.8 us (5%)
  between operations  0.64 us (1%)
    pallas_call x1, Pallas kernels, shards(): pl.pallas_call(functools.partial(kernel, n, repeats), out_shape=(jax.Shap...  55.2 us
    unnamed x2, local copies, waits for them, and re-layouts  2.8 us

profile of v5, /device:TPU:0, one launch (start us, length us, event | category | flops | bytes accessed | tf_op | source)
XLA Modules:
  0.0 58.7 jit_solution(4919496822814220510)
XLA Ops:
  0.6 55.2 %shard_map.95 = (bf16[8,128,128]{2,1,0:T(8,128)(2,1)}, f32[4]{0:T(128)}) custom-call(s32[256]{0:T(256)} %bitcast.2, s32[256]{0:T(256)} %sslot_hbm.1, s32[256]{0:T(256)} %bitcast.3, s32[256]{0:T(256)} %tslot_hbm.1, bf16[8,128,128]{2,1,0:T(8,128)(2,1)} %wave_hbm.1, bf16[4,8,128,128]{3,2,1,0:T(8,128)(2,1)} %dav_hbm.1, bf16[4,128,16,128]{3,2,1,0:T(8,128)(2,1)} %left_hbm.1, ...), custom_call_target="tpu_custom_call" | custom-call | flops 2147483648 | bytes 10485760 | tf_op jit(solution)/shard_map/pallas_call | solution.py:589
  55.9 1.7 %copy.12 = bf16[8,128,128]{2,1,0:T(8,128)(2,1)} copy(bf16[8,128,128]{2,1,0:T(8,128)(2,1)} %get-tuple-element.4) | data formatting | bytes 524288
  57.6 1.1 %copy.13 = f32[4]{0:T(128)} copy(f32[4]{0:T(128)} %get-tuple-element.5) | data formatting | bytes 32
